TPU v7x, 32 devices: a whole 2x2x4 slice. The times are simulated.
32 devices in a mesh: sec: 2 (over x), gy: 4 (over z), gx: 4 (over y, core).
Axes of the slice: x: 2, y: 2, z: 4, core: 2. Of those that a mesh axis runs over, the one named last changes fastest.
Arguments:
- fields: float32 [2, 4, 1, 768, 1536], P('sec', None, None, 'gy', 'gx'), may hold values from -6 to 6
- forcing: bfloat16 [2, 4, 1, 768, 1536], P('sec', None, None, 'gy', 'gx'), may hold values from -4 to 4
- courant: float32 [2, 1], replicated, may hold values from -0.18 to 0.18
- diffusion: float32 [4], replicated, may hold values from 0.03 to 0.08
- nest_patch: int32 [4, 4], replicated, may hold values from 0 to 35, as said below
Outputs:
- fields_out: float32 [2, 4, 1, 768, 1536], P('sec', None, None, 'gy', 'gx')
Inputs may be any that keep to these rules, and one draw needn't show every extreme that they name: Entry [i, j] names a patch of the parent device in row nest_patch[i, j] // 9 of device column j: patch row (nest_patch[i, j] % 9) // 3 and patch column nest_patch[i, j] % 3 of its 3 x 3 patches. That device row differs from i by at most one. Nests of one column lie on distinct patches; in every column some parent device lies under exactly three nests, and none under more.
All inputs are finite; a program needn't handle non-finite values.
Results may differ from a plain program's by a relative error of at most 0.0003.
Values sent between devices are 32-bit elements; how exact they have to be, the bound alone decides.
A program may use at most 128 MiB of HBM per device.

v0:
```python
import jax
import jax.numpy as jnp
from jax import lax
from jax.sharding import PartitionSpec as P

third = 1.0 / 3.0
two_thirds = 2.0 / 3.0


def extended(x, sides, width):
    for axis, dim in sides:
        devices, length = (lax.axis_size(axis), x.shape[dim])
        up = [(i, (i + 1) % devices) for i in range(devices - 1)]
        down = [(j, i) for i, j in up]
        last = lax.slice_in_dim(x, length - width, length, axis=dim)
        first = lax.slice_in_dim(x, 0, width, axis=dim)
        before = lax.ppermute(last, axis, up)
        after = lax.ppermute(first, axis, down)
        x = jnp.concatenate([before, x, after], axis=dim)
    return x


def from_behind(block, axis, distance):
    devices = range(lax.axis_size(axis))
    route = [(i - distance, i) for i in devices if i - distance in devices]
    return lax.ppermute(block, axis, route)


def as_index(value):
    return jnp.asarray(value, dtype=jnp.int32)


def stencil(padded, centre, courant, diffusion, drive):
    eastern = padded[..., 1:-1, 2:]
    western = padded[..., 1:-1, :-2]
    southern = padded[..., 2:, 1:-1]
    northern = padded[..., :-2, 1:-1]
    along_columns = courant[0].reshape(1, -1, 1, 1)
    along_rows = courant[1].reshape(1, -1, 1, 1)
    spread = diffusion.reshape(-1, 1, 1, 1)
    return (
        centre
        - 0.5 * along_columns * (eastern - western)
        - 0.5 * along_rows * (southern - northern)
        + spread * (eastern + western + southern + northern - 4.0 * centre)
        + drive
    )


def refine_edge(parent_rim):
    lower_part = parent_rim[..., :-2]
    centre_part = parent_rim[..., 1:-1]
    upper_part = parent_rim[..., 2:]
    first_third = third * lower_part + two_thirds * centre_part
    last_third = two_thirds * centre_part + third * upper_part
    stacked = jnp.stack([first_third, centre_part, last_third], axis=-1)
    return stacked.reshape(parent_rim.shape[:-1] + (3 * (parent_rim.shape[-1] - 2),))


def pack_rims(padded, row_start, col_start, patch_rows, patch_cols):
    field_count = padded.shape[0]
    level_count = padded.shape[1]
    zero = as_index(0)
    row_start = as_index(row_start)
    col_start = as_index(col_start)
    upper = lax.dynamic_slice(
        padded,
        (zero, zero, row_start, as_index(col_start + 1)),
        (field_count, level_count, 1, patch_cols),
    )[:, :, 0]
    lower = lax.dynamic_slice(
        padded,
        (zero, zero, as_index(row_start + patch_rows + 1), as_index(col_start + 1)),
        (field_count, level_count, 1, patch_cols),
    )[:, :, 0]
    western = lax.dynamic_slice(
        padded, (zero, zero, row_start, col_start), (field_count, level_count, patch_rows + 2, 1)
    )[..., 0]
    eastern = lax.dynamic_slice(
        padded,
        (zero, zero, row_start, as_index(col_start + patch_cols + 1)),
        (field_count, level_count, patch_rows + 2, 1),
    )[..., 0]
    lane_pad = ((0, 0), (0, 0), (0, patch_cols - patch_rows - 2))
    return jnp.stack([upper, lower, jnp.pad(western, lane_pad), jnp.pad(eastern, lane_pad)], axis=2)


def unpack(message, patch_rows):
    upper_row = jnp.concatenate(
        [message[..., 2, 0:1], message[..., 0, :], message[..., 3, 0:1]], axis=-1
    )
    lower_row = jnp.concatenate(
        [
            message[..., 2, patch_rows + 1 : patch_rows + 2],
            message[..., 1, :],
            message[..., 3, patch_rows + 1 : patch_rows + 2],
        ],
        axis=-1,
    )
    western = message[..., 2, : patch_rows + 2]
    eastern = message[..., 3, : patch_rows + 2]
    return (
        refine_edge(upper_row),
        refine_edge(lower_row),
        refine_edge(western),
        refine_edge(eastern),
    )


def border(field, upper, lower, western, eastern):
    stacked_rows = jnp.concatenate([upper[..., None, :], field, lower[..., None, :]], axis=-2)
    corner_zero = jnp.zeros(western.shape[:-1] + (1,), field.dtype)
    west_column = jnp.concatenate([corner_zero, western, corner_zero], axis=-1)
    east_column = jnp.concatenate([corner_zero, eastern, corner_zero], axis=-1)
    return jnp.concatenate([west_column[..., None], stacked_rows, east_column[..., None]], axis=-1)


def nest_steps(field, drive_fine, edges_start, edges_end, courant, diffusion):
    fine_spread = diffusion * 3.0
    fine_force = drive_fine.astype(jnp.float32) / 3.0
    for substep in range(3):
        fraction = substep / 3.0
        upper, lower, western, eastern = [
            start_edge + fraction * (end_edge - start_edge)
            for start_edge, end_edge in zip(edges_start, edges_end)
        ]
        padded = border(field, upper, lower, western, eastern)
        field = stencil(padded, field, courant, fine_spread, fine_force)
    return field


def tile_faces(field):
    return extended(field[None], (("gy", 3), ("gx", 4)), 1)[0]


def on_device(fields, forcing, courant, diffusion, nest_patch):
    own_tile = fields[0]
    own_drive = forcing[0]
    field_count, level_count, tile_height, tile_width = own_tile.shape
    patch_rows = tile_height // 3
    patch_cols = tile_width // 3
    rows_total = nest_patch.shape[0]
    own_row = lax.axis_index("gy")
    own_column = lax.axis_index("gx")
    is_parent = lax.axis_index("sec") == 0
    placed = lax.dynamic_index_in_dim(nest_patch, own_column, axis=1, keepdims=False)
    padded_before = tile_faces(own_tile)
    advanced = lax.cond(
        is_parent,
        lambda: stencil(padded_before, own_tile, courant, diffusion, own_drive.astype(jnp.float32)),
        lambda: own_tile,
    )
    padded_after = tile_faces(advanced)

    def role_message(member):
        target_row = jnp.clip(own_row + member - 1, 0, rows_total - 1)
        slot = lax.dynamic_index_in_dim(placed, target_row, keepdims=False) % 9
        row_start = slot // 3 * patch_rows
        col_start = slot % 3 * patch_cols
        return jnp.stack(
            [
                pack_rims(padded_before, row_start, col_start, patch_rows, patch_cols),
                pack_rims(padded_after, row_start, col_start, patch_rows, patch_cols),
            ],
            axis=2,
        )

    roles = jnp.stack([role_message(member) for member in range(3)], axis=0)
    source_row = lax.dynamic_index_in_dim(placed, own_row, keepdims=False) // 9
    offset = source_row - own_row
    pick_entry = 2 * (offset + 1)
    crossed = from_behind(roles, "sec", 1)
    spread_rims = extended(crossed, (("gy", 0),), 1)
    received = lax.dynamic_index_in_dim(spread_rims, pick_entry, axis=0, keepdims=False)
    edges_start = unpack(received[:, :, 0], patch_rows)
    edges_end = unpack(received[:, :, 1], patch_rows)

    def run_nest():
        finished = nest_steps(own_tile, own_drive, edges_start, edges_end, courant, diffusion)
        averaged = finished.reshape(field_count, level_count, patch_rows, 3, patch_cols, 3).mean(
            axis=(3, 5)
        )
        return (finished, averaged)

    def keep_parent():
        return (
            own_tile,
            jnp.zeros((field_count, level_count, patch_rows, patch_cols), jnp.float32),
        )

    finished, averaged = lax.cond(is_parent, keep_parent, run_nest)
    outgoing = jnp.stack(
        [jnp.where(offset + 1 == member, averaged, 0.0) for member in range(3)], axis=0
    )
    spread_back = extended(outgoing, (("gy", 0),), 1)
    arrived = from_behind(spread_back[0:5:2], "sec", -1)
    slot_index = jnp.arange(9, dtype=jnp.int32)
    patch_choice = jnp.full((9,), -1, jnp.int32)
    for member in range(3):
        source = own_row + member - 1
        inside_rows = (source >= 0) & (source < rows_total)
        entry = lax.dynamic_index_in_dim(
            placed, jnp.clip(source, 0, rows_total - 1), keepdims=False
        )
        valid = inside_rows & (entry // 9 == own_row)
        patch_choice = jnp.where(valid & (slot_index == entry % 9), member, patch_choice)
    patch_grid = patch_choice.reshape(1, 1, 3, 1, 3, 1)
    blocks = advanced.reshape(field_count, level_count, 3, patch_rows, 3, patch_cols)
    for member in range(3):
        blocks = jnp.where(patch_grid == member, arrived[member][:, :, None, :, None, :], blocks)
    corrected = blocks.reshape(field_count, level_count, tile_height, tile_width)
    result = jnp.where(is_parent, corrected, finished)
    return result[None]


def solution(mesh):
    return jax.shard_map(
        on_device,
        mesh=mesh,
        in_specs=(
            P("sec", None, None, "gy", "gx"),
            P("sec", None, None, "gy", "gx"),
            P(),
            P(),
            P(),
        ),
        out_specs=P("sec", None, None, "gy", "gx"),
        check_vma=False,
    )
```

profile of v0, /device:TPU:0, one launch (start us, length us, event | category | flops | bytes accessed | tf_op | source)
XLA Modules:
  0.0 189.0 jit_solution(14688045110156929448)
XLA Ops:
  0.0 2.4 %copy.101 = f32[1,4,1,192,384]{4,3,2,1,0:T(8,128)} copy(f32[1,4,1,192,384]{4,3,2,1,0:T(8,128)} %param.9) | data formatting | bytes 2359296
  2.4 0.8 fusion.43
  3.2 4.9 %collective-permute-start = (f32[1,4,1,1,384]{4,3,2,1,0:T(1,128)S(1)}, f32[1,4,1,1,384]{4,3,2,1,0:T(1,128)S(1)}, u32[]{:S(2)}, u32[]{:S(2)}) collective-permute-start(f32[1,4,1,1,384]{4,3,2,1,0:T(1,128)S(1)} %get-tuple-element.160), channel_id=1, source_target_pairs={{0,4},{4,8},{8,12},{1,5},{5,9},{9,13},{2,6},{6,10},{10,14},{3,7},{... | collective-permute-start | bytes 18440 | tf_op jit(solution)/shard_map/ppermute | solution.py:17
  8.1 1.3 collective-permute-start.1
  9.5 0.7 fusion.45
  12.1 0.0 collective-permute-done
  12.1 1.5 collective-permute-done.1
  13.7 1.3 pad_maximum_fusion.43
  15.0 1.3 collective-permute-start.2
  16.3 1.3 collective-permute-start.3
  17.7 0.0 copy-start
  17.8 0.0 copy-start.1
  17.8 0.0 copy-start.3
  17.8 4.0 %collective-permute-done.3 = f32[1,4,1,194,1]{4,3,2,1,0:T(8,128)} collective-permute-done((f32[1,4,1,194,1]{4,3,2,1,0:T(8,128)S(1)}, f32[1,4,1,194,1]{4,3,2,1,0:T(8,128)}, u32[]{:S(2)}, u32[]{:S(2)}) %collective-permute-start.3) | collective-permute-done | bytes 3136 | tf_op jit(solution)/shard_map/ppermute | solution.py:18
  21.8 2.1 %pad_maximum_fusion.36 = f32[1,4,1,194,386]{4,3,2,1,0:T(8,128)S(1)} fusion(f32[1,4,1,194,1]{4,3,2,1,0:T(8,128)} %collective-permute-done.3, f32[1,4,1,1,384]{4,3,2,1,0:T(1,128)S(1)} %collective-permute-done.1, f32[1,4,1,192,384]{4,3,2,1,0:T(8,128)} %copy.101, f32[1,4,1,1,384]{4,3,2,1,0:T(1,128)S(1)} %collective-permute-done, ...), kind=kLoop, calls=%fused_computation.61 | loop fusion | flops 1198144 | bytes 2396288 | tf_op jit(solution)/shard_map/concatenate | solution.py:19
  23.9 4.4 %conditional.2 = (f32[4,1,192,384]{3,2,0,1:T(8,128)S(1)}) conditional(s32[]{:T(128)} %convert_element_type.23, f32[4,1,192,384]{3,2,0,1:T(8,128)} %bitcast.34, (f32[2,1]{0,1:T(1,128)S(1)}, f32[1,4,1,194,386]{4,3,2,1,0:T(8,128)S(1)}, f32[4,1,192,384]{3,2,0,1:T(8,128)}, f32[4]{0:T(128)S(1)}, bf16[4,1,192,384]{3,2,0,1:T(8,128)(2,1)S(1)}) %tuple.115), branch_computations={%region_0.1_spmd, %region_1.2_spmd} | conditional | flops 4423682 | bytes 7667784 | solution.py:148
  24.0 0.6 fusion.40
  25.9 2.4 %convert_add_fusion = f32[4,1,192,384]{3,2,0,1:T(8,128)S(1)} fusion(bf16[4,1,192,384]{3,2,0,1:T(8,128)(2,1)S(1)} %get-tuple-element.49, f32[4,1,192,384]{3,2,0,1:T(8,128)} %get-tuple-element.45, f32[4,1,194,386]{3,2,0,1:T(8,128)S(1)} %bitcast.267, f32[4]{0:T(128)S(1)} %get-tuple-element.48, f32[]{:T(128)} %bitcast.2, f32[]{:T(128)} %bitcast), kind=kLoop, calls=%fused_computation | loop fusion | flops 4423680 | bytes 7667736 | tf_op jit(solution)/shard_map/cond/branch_1_fun/add | solution.py:42
  28.4 3.5 %collective-permute-start.4 = (f32[1,4,1,1,384]{4,3,1,2,0:T(1,128)S(1)}, f32[1,4,1,1,384]{4,3,1,2,0:T(1,128)S(1)}, u32[]{:S(2)}, u32[]{:S(2)}) collective-permute-start(f32[1,4,1,1,384]{4,3,1,2,0:T(1,128)S(1)} %get-tuple-element.158), channel_id=1, source_target_pairs={{0,4},{4,8},{8,12},{1,5},{5,9},{9,13},{2,6},{6,10},{10,14},{3,7},{... | collective-permute-start | bytes 18440 | tf_op jit(solution)/shard_map/ppermute | solution.py:17
  31.9 1.3 collective-permute-start.5
  33.2 0.8 dynamic-slice_reduce_fusion.11
  34.0 0.1 constant_dynamic-slice_fusion.11
  34.2 3.2 %collective-permute-done.5 = f32[1,4,1,1,384]{4,3,1,2,0:T(1,128)S(1)} collective-permute-done((f32[1,4,1,1,384]{4,3,1,2,0:T(1,128)S(1)}, f32[1,4,1,1,384]{4,3,1,2,0:T(1,128)S(1)}, u32[]{:S(2)}, u32[]{:S(2)}) %collective-permute-start.5) | collective-permute-done | bytes 6176 | tf_op jit(solution)/shard_map/ppermute | solution.py:18
  37.4 0.2 pad_maximum_fusion.40
  37.6 6.6 %collective-permute-start.6 = (f32[1,4,1,194,1]{4,3,1,2,0:T(8,128)S(1)}, f32[1,4,1,194,1]{4,3,1,2,0:T(8,128)S(1)}, u32[]{:S(2)}, u32[]{:S(2)}) collective-permute-start(f32[1,4,1,194,1]{4,3,1,2,0:T(8,128)S(1)} %get-tuple-element.154), channel_id=1, source_target_pairs={{0,1},{1,2},{2,3},{4,5},{5,6},{6,7},{8,9},{9,10},{10,11},{12,13},{... | collective-permute-start | bytes 9320 | tf_op jit(solution)/shard_map/ppermute | solution.py:17
  44.2 1.3 collective-permute-start.7
  45.5 0.0 collective-permute-done.6
  45.5 3.0 %collective-permute-done.7 = f32[1,4,1,194,1]{4,3,1,2,0:T(8,128)S(1)} collective-permute-done((f32[1,4,1,194,1]{4,3,1,2,0:T(8,128)S(1)}, f32[1,4,1,194,1]{4,3,1,2,0:T(8,128)S(1)}, u32[]{:S(2)}, u32[]{:S(2)}) %collective-permute-start.7) | collective-permute-done | bytes 3136 | tf_op jit(solution)/shard_map/ppermute | solution.py:18
  48.5 0.7 pad_maximum_fusion.37
  49.2 0.8 dynamic-slice_reduce_fusion.9
  49.9 0.1 constant_dynamic-slice_fusion.9
  50.2 1.3 collective-permute-start.8
  51.5 1.7 collective-permute-done.8
  53.3 1.3 collective-permute-start.10
  54.5 4.5 %collective-permute-start.9 = (f32[1,4,1,2,4,128]{5,1,4,3,2,0:T(4,128)S(1)}, f32[1,4,1,2,4,128]{5,1,4,3,2,0:T(4,128)S(1)}, u32[]{:S(2)}, u32[]{:S(2)}) collective-permute-start(f32[1,4,1,2,4,128]{5,1,4,3,2,0:T(4,128)S(1)} %get-tuple-element.166), channel_id=1, source_target_pairs={{0,4},{4,8},{8,12},{1,5},{5,9},{9,13},{2,6},{6,10},{10,14},{3,7},{... | collective-permute-start | bytes 49160 | tf_op jit(solution)/shard_map/ppermute | solution.py:17
  60.8 0.0 collective-permute-done.10
  60.8 0.0 collective-permute-done.9
  60.8 0.1 slice_bitcast_fusion.10
  60.9 0.1 slice_bitcast_fusion.12
  61.0 0.1 add_bitcast_fusion.7
  61.1 0.1 add_bitcast_fusion.9
  61.2 0.1 add_bitcast_fusion.11
  61.2 0.1 add_bitcast_fusion.13
  61.4 0.1 fusion.15
  61.4 0.1 fusion.21
  61.5 0.1 fusion.27
  61.6 0.1 fusion.33
  61.7 0.2 conditional.3
  61.9 3.9 %collective-permute-start.11 = (f32[1,4,1,64,128]{4,3,1,2,0:T(8,128)S(1)}, f32[1,4,1,64,128]{4,3,1,2,0:T(8,128)S(1)}, u32[]{:S(2)}, u32[]{:S(2)}) collective-permute-start(f32[1,4,1,64,128]{4,3,1,2,0:T(8,128)S(1)} %select_bitcast_fusion.2), channel_id=1, source_target_pairs={{0,4},{4,8},{8,12},{1,5},{5,9},{9,13},{2,6},{6,10},{10,14},{3,7},{... | collective-permute-start | bytes 393224 | tf_op jit(solution)/shard_map/ppermute | solution.py:17
  65.9 2.5 %collective-permute-done.11 = f32[1,4,1,64,128]{4,3,1,2,0:T(8,128)S(1)} collective-permute-done((f32[1,4,1,64,128]{4,3,1,2,0:T(8,128)S(1)}, f32[1,4,1,64,128]{4,3,1,2,0:T(8,128)S(1)}, u32[]{:S(2)}, u32[]{:S(2)}) %collective-permute-start.11) | collective-permute-done | bytes 131104 | tf_op jit(solution)/shard_map/ppermute | solution.py:17
  68.4 1.3 collective-permute-start.12
  69.8 6.0 %collective-permute-done.12 = f32[1,4,1,64,128]{4,3,1,2,0:T(8,128)S(1)} collective-permute-done((f32[1,4,1,64,128]{4,3,1,2,0:T(8,128)S(1)}, f32[1,4,1,64,128]{4,3,1,2,0:T(8,128)S(1)}, u32[]{:S(2)}, u32[]{:S(2)}) %collective-permute-start.12) | collective-permute-done | bytes 131104 | tf_op jit(solution)/shard_map/ppermute | solution.py:18
  75.8 1.3 collective-permute-start.13
  80.8 0.1 broadcast_in_dim.135
  81.0 0.1 broadcast_in_dim.129
  81.2 0.1 broadcast_in_dim.121
  81.4 99.0 %collective-permute-done.13 = f32[3,4,1,64,128]{4,3,1,2,0:T(8,128)S(1)} collective-permute-done((f32[3,4,1,64,128]{4,3,1,2,0:T(8,128)S(1)}, f32[3,4,1,64,128]{4,3,1,2,0:T(8,128)S(1)}, u32[]{:S(2)}, u32[]{:S(2)}) %collective-permute-start.13) | collective-permute-done | bytes 393248 | tf_op jit(solution)/shard_map/ppermute | solution.py:26
  180.4 0.3 broadcast_in_dim.127
  180.7 1.5 broadcast_in_dim.128
  182.2 0.3 broadcast_in_dim.133
  182.4 1.5 broadcast_in_dim.134
  183.9 0.3 broadcast_in_dim.139
  184.2 1.5 broadcast_in_dim.140
  185.7 3.3 %select_bitcast_fusion = f32[1,4,1,192,384]{4,3,2,1,0:T(8,128)} fusion(f32[4,1,192,384]{3,2,0,1:T(8,128)} %get-tuple-element.65, f32[4,1,192,384]{3,2,0,1:T(8,128)} %broadcast_in_dim.128, f32[4,1,192,384]{3,2,0,1:T(8,128)} %broadcast_in_dim.134, f32[4,1,192,384]{3,2,0,1:T(8,128)} %broadcast_in_dim.140, f32[4,1,192,384]{3,2,0,1:T(8,128)S(1)} %get-tuple-element.231, ...), kind=kLoop, calls=%fused_computation.63 | loop fusion | flops 1179648 | bytes 7299073 | tf_op jit(solution)/shard_map/broadcast_in_dim | solution.py:213
  (53 shorter events, 0.5 us)
Async XLA Ops:
  0.0 9.5 %copy-start.2 = (s32[4,4]{1,0:T(4,128)S(1)}, s32[4,4]{1,0:T(4,128)}, u32[]{:S(2)}) copy-start(s32[4,4]{1,0:T(4,128)} %param.13) | copy-start | bytes 196
  3.2 8.9 %collective-permute-start = (f32[1,4,1,1,384]{4,3,2,1,0:T(1,128)S(1)}, f32[1,4,1,1,384]{4,3,2,1,0:T(1,128)S(1)}, u32[]{:S(2)}, u32[]{:S(2)}) collective-permute-start(f32[1,4,1,1,384]{4,3,2,1,0:T(1,128)S(1)} %get-tuple-element.160), channel_id=1, source_target_pairs={{0,4},{4,8},{8,12},{1,5},{5,9},{9,13},{2,6},{6,10},{10,14},{3,7},{... | collective-permute-start | bytes 18440 | tf_op jit(solution)/shard_map/ppermute | solution.py:17
  8.1 5.5 %collective-permute-start.1 = (f32[1,4,1,1,384]{4,3,2,1,0:T(1,128)S(1)}, f32[1,4,1,1,384]{4,3,2,1,0:T(1,128)S(1)}, u32[]{:S(2)}, u32[]{:S(2)}) collective-permute-start(f32[1,4,1,1,384]{4,3,2,1,0:T(1,128)S(1)} %get-tuple-element.161), channel_id=1, source_target_pairs={{4,0},{8,4},{12,8},{5,1},{9,5},{13,9},{6,2},{10,6},{14,10},{7,3},{... | collective-permute-start | bytes 18440 | tf_op jit(solution)/shard_map/ppermute | solution.py:18
  15.0 2.8 %collective-permute-start.2 = (f32[1,4,1,194,1]{4,3,2,1,0:T(8,128)S(1)}, f32[1,4,1,194,1]{4,3,2,1,0:T(8,128)S(1)}, u32[]{:S(2)}, u32[]{:S(2)}) collective-permute-start(f32[1,4,1,194,1]{4,3,2,1,0:T(8,128)S(1)} %get-tuple-element.156), channel_id=1, source_target_pairs={{0,1},{1,2},{2,3},{4,5},{5,6},{6,7},{8,9},{9,10},{10,11},{12,13},{... | collective-permute-start | bytes 9320 | tf_op jit(solution)/shard_map/ppermute | solution.py:17
  16.3 5.5 %collective-permute-start.3 = (f32[1,4,1,194,1]{4,3,2,1,0:T(8,128)S(1)}, f32[1,4,1,194,1]{4,3,2,1,0:T(8,128)}, u32[]{:S(2)}, u32[]{:S(2)}) collective-permute-start(f32[1,4,1,194,1]{4,3,2,1,0:T(8,128)S(1)} %get-tuple-element.157), channel_id=1, source_target_pairs={{1,0},{2,1},{3,2},{5,4},{6,5},{7,6},{9,8},{10,9},{11,10},{13,12},{... | collective-permute-start | bytes 9320 | tf_op jit(solution)/shard_map/ppermute | solution.py:18
  17.7 6.2 %copy-start = (bf16[1,4,1,192,384]{4,3,2,1,0:T(8,128)(2,1)S(1)}, bf16[1,4,1,192,384]{4,3,2,1,0:T(8,128)(2,1)}, u32[]{:S(2)}) copy-start(bf16[1,4,1,192,384]{4,3,2,1,0:T(8,128)(2,1)} %param.10) | copy-start | bytes 1769476
  17.8 6.2 %copy-start.1 = (f32[2,1]{0,1:T(1,128)S(1)}, f32[2,1]{0,1:T(1,128)}, u32[]{:S(2)}) copy-start(f32[2,1]{0,1:T(1,128)} %param.11) | copy-start | bytes 28
  17.8 6.2 %copy-start.3 = (f32[4]{0:T(128)S(1)}, f32[4]{0:T(128)}, u32[]{:S(2)}) copy-start(f32[4]{0:T(128)} %param.12) | copy-start | bytes 52
  28.4 5.8 %collective-permute-start.4 = (f32[1,4,1,1,384]{4,3,1,2,0:T(1,128)S(1)}, f32[1,4,1,1,384]{4,3,1,2,0:T(1,128)S(1)}, u32[]{:S(2)}, u32[]{:S(2)}) collective-permute-start(f32[1,4,1,1,384]{4,3,1,2,0:T(1,128)S(1)} %get-tuple-element.158), channel_id=1, source_target_pairs={{0,4},{4,8},{8,12},{1,5},{5,9},{9,13},{2,6},{6,10},{10,14},{3,7},{... | collective-permute-start | bytes 18440 | tf_op jit(solution)/shard_map/ppermute | solution.py:17
  31.9 5.5 %collective-permute-start.5 = (f32[1,4,1,1,384]{4,3,1,2,0:T(1,128)S(1)}, f32[1,4,1,1,384]{4,3,1,2,0:T(1,128)S(1)}, u32[]{:S(2)}, u32[]{:S(2)}) collective-permute-start(f32[1,4,1,1,384]{4,3,1,2,0:T(1,128)S(1)} %get-tuple-element.159), channel_id=1, source_target_pairs={{4,0},{8,4},{12,8},{5,1},{9,5},{13,9},{6,2},{10,6},{14,10},{7,3},{... | collective-permute-start | bytes 18440 | tf_op jit(solution)/shard_map/ppermute | solution.py:18
  37.6 7.9 %collective-permute-start.6 = (f32[1,4,1,194,1]{4,3,1,2,0:T(8,128)S(1)}, f32[1,4,1,194,1]{4,3,1,2,0:T(8,128)S(1)}, u32[]{:S(2)}, u32[]{:S(2)}) collective-permute-start(f32[1,4,1,194,1]{4,3,1,2,0:T(8,128)S(1)} %get-tuple-element.154), channel_id=1, source_target_pairs={{0,1},{1,2},{2,3},{4,5},{5,6},{6,7},{8,9},{9,10},{10,11},{12,13},{... | collective-permute-start | bytes 9320 | tf_op jit(solution)/shard_map/ppermute | solution.py:17
  44.2 4.3 %collective-permute-start.7 = (f32[1,4,1,194,1]{4,3,1,2,0:T(8,128)S(1)}, f32[1,4,1,194,1]{4,3,1,2,0:T(8,128)S(1)}, u32[]{:S(2)}, u32[]{:S(2)}) collective-permute-start(f32[1,4,1,194,1]{4,3,1,2,0:T(8,128)S(1)} %get-tuple-element.155), channel_id=1, source_target_pairs={{1,0},{2,1},{3,2},{5,4},{6,5},{7,6},{9,8},{10,9},{11,10},{13,12},{... | collective-permute-start | bytes 9320 | tf_op jit(solution)/shard_map/ppermute | solution.py:18
  50.2 3.0 %collective-permute-start.8 = (f32[3,4,1,2,4,128]{5,1,4,3,2,0:T(4,128)S(1)}, f32[3,4,1,2,4,128]{5,1,4,3,2,0:T(4,128)S(1)}, u32[]{:S(2)}, u32[]{:S(2)}) collective-permute-start(f32[3,4,1,2,4,128]{5,1,4,3,2,0:T(4,128)S(1)} %pad_maximum_fusion.44), channel_id=1, source_target_pairs={{0,16},{1,17},{2,18},{3,19},{4,20},{5,21},{6,22},{7,23},{8,24},{9,... | collective-permute-start | bytes 147464 | tf_op jit(solution)/shard_map/ppermute | solution.py:26
  53.3 7.5 %collective-permute-start.10 = (f32[1,4,1,2,4,128]{5,1,4,3,2,0:T(4,128)S(1)}, f32[1,4,1,2,4,128]{5,1,4,3,2,0:T(4,128)S(1)}, u32[]{:S(2)}, u32[]{:S(2)}) collective-permute-start(f32[1,4,1,2,4,128]{5,1,4,3,2,0:T(4,128)S(1)} %get-tuple-element.165), channel_id=1, source_target_pairs={{4,0},{8,4},{12,8},{5,1},{9,5},{13,9},{6,2},{10,6},{14,10},{7,3},{... | collective-permute-start | bytes 49160 | tf_op jit(solution)/shard_map/ppermute | solution.py:18
  54.5 6.2 %collective-permute-start.9 = (f32[1,4,1,2,4,128]{5,1,4,3,2,0:T(4,128)S(1)}, f32[1,4,1,2,4,128]{5,1,4,3,2,0:T(4,128)S(1)}, u32[]{:S(2)}, u32[]{:S(2)}) collective-permute-start(f32[1,4,1,2,4,128]{5,1,4,3,2,0:T(4,128)S(1)} %get-tuple-element.166), channel_id=1, source_target_pairs={{0,4},{4,8},{8,12},{1,5},{5,9},{9,13},{2,6},{6,10},{10,14},{3,7},{... | collective-permute-start | bytes 49160 | tf_op jit(solution)/shard_map/ppermute | solution.py:17
  61.9 6.4 %collective-permute-start.11 = (f32[1,4,1,64,128]{4,3,1,2,0:T(8,128)S(1)}, f32[1,4,1,64,128]{4,3,1,2,0:T(8,128)S(1)}, u32[]{:S(2)}, u32[]{:S(2)}) collective-permute-start(f32[1,4,1,64,128]{4,3,1,2,0:T(8,128)S(1)} %select_bitcast_fusion.2), channel_id=1, source_target_pairs={{0,4},{4,8},{8,12},{1,5},{5,9},{9,13},{2,6},{6,10},{10,14},{3,7},{... | collective-permute-start | bytes 393224 | tf_op jit(solution)/shard_map/ppermute | solution.py:17
  68.4 7.3 %collective-permute-start.12 = (f32[1,4,1,64,128]{4,3,1,2,0:T(8,128)S(1)}, f32[1,4,1,64,128]{4,3,1,2,0:T(8,128)S(1)}, u32[]{:S(2)}, u32[]{:S(2)}) collective-permute-start(f32[1,4,1,64,128]{4,3,1,2,0:T(8,128)S(1)} %get-tuple-element.116), channel_id=1, source_target_pairs={{4,0},{8,4},{12,8},{5,1},{9,5},{13,9},{6,2},{10,6},{14,10},{7,3},{... | collective-permute-start | bytes 393224 | tf_op jit(solution)/shard_map/ppermute | solution.py:18
  75.8 104.6 %collective-permute-start.13 = (f32[3,4,1,64,128]{4,3,1,2,0:T(8,128)S(1)}, f32[3,4,1,64,128]{4,3,1,2,0:T(8,128)S(1)}, u32[]{:S(2)}, u32[]{:S(2)}) collective-permute-start(f32[3,4,1,64,128]{4,3,1,2,0:T(8,128)S(1)} %slice.288), channel_id=1, source_target_pairs={{16,0},{17,1},{18,2},{19,3},{20,4},{21,5},{22,6},{23,7},{24,8},{25... | collective-permute-start | bytes 1179656 | tf_op jit(solution)/shard_map/ppermute | solution.py:26
where the time goes:
time: 191 us; the launch traced here: 189 us
  waiting for transfers between devices  121 us (63%)
  starting transfers between devices  35.1 us (18%)
  local copies, waits for them, and re-layouts  12.4 us (6%)
  other arithmetic  10.9 us (6%)
  between operations  8.1 us (4%)
    ppermute x2, waiting for transfers between devices, from_behind(): return lax.ppermute(block, axis, route)  101 us
    ppermute x6, starting transfers between devices, extended(): before = lax.ppermute(last, axis, up)  24.8 us
    ppermute x6, waiting for transfers between devices, extended(): after = lax.ppermute(first, axis, down)  17.7 us
    ppermute x6, starting transfers between devices, extended(): after = lax.ppermute(first, axis, down)  7.74 us
    broadcast_in_dim x10, local copies, waits for them, and re-layouts, on_device(): jnp.where(patch_grid == member, arrived[member][:, :, None, :, None, :],...  5.67 us
  transfers between devices with their start and end apart: 14, of which 8 were waited for; matrix products, arithmetic and copies ran while one was open for 1% of the time, Pallas kernels for 0%

commit v1 on v0

v1 whole, which is shorter than its diff:
```python
import functools

import jax
import jax.numpy as jnp
from jax import lax
from jax.experimental import pallas as pl
from jax.experimental.pallas import tpu as pltpu
from jax.sharding import PartitionSpec as P

MESH = pl.DeviceIdType.MESH
third = 1.0 / 3.0
PAD_ROWS = 8
LANES = 128
DIRECTIONS = ((-1, 0), (1, 0), (0, -1), (0, 1), (-1, -1), (-1, 1), (1, -1), (1, 1))


def all_of(terms):
    result = terms[0]
    for term in terms[1:]:
        result = jnp.logical_and(result, term)
    return result


def kernel(
    rows_total,
    cols_total,
    fields_hbm,
    forcing_hbm,
    courant,
    diffusion,
    nest_patch,
    out_ref,
    ext,
    force,
    col_send,
    col_recv,
    rim_rows,
    rim_send,
    rim_recv,
    block_send,
    block_recv,
    fold,
    load_sem,
    halo_send_sem,
    halo_recv_sem,
    rim_send_sem,
    rim_recv_sem,
    up_send_sem,
    up_recv_sem,
    side_send_sem,
    side_recv_sem,
):
    count, height, width = out_ref.shape
    patch_rows, patch_cols = height // 3, width // 3
    sec = lax.axis_index("sec")
    row = lax.axis_index("gy")
    col = lax.axis_index("gx")
    is_parent = sec == 0
    is_nest = sec == 1
    top, bottom = PAD_ROWS, PAD_ROWS + height
    left, right = LANES, LANES + width

    load_fields = pltpu.make_async_copy(
        fields_hbm, ext.at[0, :, top:bottom, left:right], load_sem.at[0]
    )
    load_force = pltpu.make_async_copy(forcing_hbm, force, load_sem.at[1])
    load_fields.start()
    load_force.start()

    def there(dy, dx=0):
        terms = []
        if dy < 0:
            terms.append(row > 0)
        if dy > 0:
            terms.append(row < rows_total - 1)
        if dx < 0:
            terms.append(col > 0)
        if dx > 0:
            terms.append(col < cols_total - 1)
        return all_of(terms) if terms else row >= 0

    barrier = pltpu.get_barrier_semaphore()

    def greet(condition, where):
        @pl.when(condition)
        def _():
            pl.semaphore_signal(barrier, inc=1, device_id=where, device_id_type=MESH)

    for dy, dx in DIRECTIONS:
        greet(all_of([is_parent, there(dy, dx)]), (sec, row + dy, col + dx))
    for dy in (-1, 0, 1):
        greet(there(dy), (1 - sec, row + dy, col))
    def one_if(condition):
        return jnp.where(condition, jnp.int32(1), jnp.int32(0))

    in_row = one_if(there(0, -1)) + one_if(there(0, 1)) + 1
    in_column = one_if(there(-1)) + one_if(there(1)) + 1
    pl.semaphore_wait(barrier, in_column + (1 - sec) * (in_row * in_column - 1))
    load_fields.wait()

    lane = lax.broadcasted_iota(jnp.int32, (1, LANES), 1)
    wide_lane = lax.broadcasted_iota(jnp.int32, (1, width), 1)
    half_x = 0.5 * courant[0, 0]
    half_y = 0.5 * courant[1, 0]
    chunk = 32

    def stencil_field(index, source, west_of, east_of, spread, drive_scale, store):
        for start in range(0, height, chunk):
            rows = slice(top + start, top + start + chunk)
            centre = source[rows, left:right]
            north = source[top + start - 1 : top + start - 1 + chunk, left:right]
            south = source[top + start + 1 : top + start + 1 + chunk, left:right]
            west = jnp.where(wide_lane == 0, west_of(start), pltpu.roll(centre, 1, 1))
            east = jnp.where(wide_lane == width - 1, east_of(start), pltpu.roll(centre, width - 1, 1))
            drive = force[index, start : start + chunk].astype(jnp.float32)
            value = (
                (1.0 - 4.0 * spread) * centre
                + (spread - half_x) * east
                + (spread + half_x) * west
                + (spread - half_y) * south
                + (spread + half_y) * north
                + drive_scale * drive
            )
            store(start, value)

    @pl.when(is_parent)
    def _parent():
        def halo_copy(phase, direction):
            dy, dx = DIRECTIONS[direction]
            where = (sec, row + dy, col + dx)
            sems = (halo_send_sem.at[phase, direction], halo_recv_sem.at[phase, direction])
            if dy == 0:
                side = 0 if dx < 0 else 1
                source = col_send.at[phase, side]
                target = col_recv.at[phase, 1 - side]
            else:
                rows_from = slice(top, top + PAD_ROWS) if dy < 0 else slice(bottom - PAD_ROWS, bottom)
                rows_to = slice(bottom, bottom + PAD_ROWS) if dy < 0 else slice(0, top)
                if dx == 0:
                    lanes_from = lanes_to = slice(left, right)
                elif dx < 0:
                    lanes_from, lanes_to = slice(left, left + LANES), slice(right, right + LANES)
                else:
                    lanes_from, lanes_to = slice(right - LANES, right), slice(0, left)
                source = ext.at[phase, :, rows_from, lanes_from]
                target = ext.at[phase, :, rows_to, lanes_to]
            return pltpu.make_async_remote_copy(
                src_ref=source,
                dst_ref=target,
                send_sem=sems[0],
                recv_sem=sems[1],
                device_id=where,
                device_id_type=MESH,
            )

        def start_exchange(phase):
            for direction in (0, 1, 4, 5, 6, 7):

                @pl.when(there(*DIRECTIONS[direction]))
                def _():
                    halo_copy(phase, direction).start()

            packed = jnp.zeros((height, LANES), jnp.float32)
            for index in range(count):
                first = ext[phase, index, top:bottom, left : left + LANES]
                last = ext[phase, index, top:bottom, right - LANES : right]
                packed = jnp.where(lane == index, first[:, 0:1], packed)
                packed = jnp.where(lane == 8 + index, last[:, LANES - 1 : LANES], packed)
            tall = col_send.shape[-1]
            packed = jnp.concatenate([packed, jnp.zeros((tall - height, LANES), jnp.float32)], axis=0)
            flat = packed.T
            col_send[phase, 0] = flat[0:8]
            col_send[phase, 1] = flat[8:16]
            for direction in (2, 3):

                @pl.when(there(*DIRECTIONS[direction]))
                def _():
                    halo_copy(phase, direction).start()

            for direction in range(8):
                dy, dx = DIRECTIONS[direction]

                @pl.when(jnp.logical_not(there(-dy, -dx)))
                def _():
                    if dy == 0:
                        side = 1 if dx < 0 else 0
                        col_recv[phase, side] = jnp.zeros(col_recv.shape[2:], jnp.float32)
                    else:
                        rows_to = slice(bottom, bottom + PAD_ROWS) if dy < 0 else slice(0, top)
                        if dx == 0:
                            lanes_to = slice(left, right)
                        elif dx < 0:
                            lanes_to = slice(right, right + LANES)
                        else:
                            lanes_to = slice(0, left)
                        ext[phase, :, rows_to, lanes_to] = jnp.zeros(
                            (count, PAD_ROWS, lanes_to.stop - lanes_to.start), jnp.float32
                        )

        def end_exchange(phase):
            for direction in range(8):
                dy, dx = DIRECTIONS[direction]

                @pl.when(there(-dy, -dx))
                def _():
                    halo_copy(phase, direction).wait_recv()

            both = jnp.concatenate(
                [
                    col_recv[phase, 0],
                    col_recv[phase, 1],
                    jnp.zeros((LANES - 16, col_recv.shape[-1]), jnp.float32),
                ],
                axis=0,
            )
            columns = both.T
            for index in range(count):
                for side, base in ((0, 0), (1, 8)):
                    value = columns[0:height, base + index : base + index + 1]
                    begin = 0 if side == 0 else right
                    ext[phase, index, top:bottom, begin : begin + LANES] = jnp.broadcast_to(
                        value, (height, LANES)
                    )

        start_exchange(0)
        load_force.wait()
        end_exchange(0)

        def advance(index, carry):
            source = ext.at[0, index]

            def store(start, value):
                ext[1, index, top + start : top + start + chunk, left:right] = value

            stencil_field(
                index,
                source,
                lambda start: source[top + start : top + start + chunk, 0:LANES][:, LANES - 1 : LANES],
                lambda start: source[top + start : top + start + chunk, right : right + LANES][:, 0:1],
                diffusion[index],
                1.0,
                store,
            )
            return carry

        lax.fori_loop(0, count, advance, 0)
        start_exchange(1)
        end_exchange(1)

        def rim_copy(member):
            return pltpu.make_async_remote_copy(
                src_ref=rim_send.at[member],
                dst_ref=rim_recv.at[2 - member],
                send_sem=rim_send_sem.at[member],
                recv_sem=rim_recv_sem.at[2 - member],
                device_id=(1 - sec, row + member - 1, col),
                device_id_type=MESH,
            )

        full = ext.shape[2]
        stretch = 2 * LANES
        packed = jnp.zeros((full, LANES), jnp.float32)
        for index in range(count):
            for phase in range(2):
                place = 2 * index + phase
                for part in range(3):
                    above = top + part * patch_rows - 1
                    below = top + (part + 1) * patch_rows
                    rim_rows[part, place : place + 1] = ext[phase, index, above : above + 1, left:right]
                    rim_rows[part, 8 + place : 9 + place] = ext[phase, index, below : below + 1, left:right]
                    begin = part * patch_cols
                    western = ext[phase, index, :, begin : begin + LANES]
                    begin = left + (part + 1) * patch_cols
                    eastern = ext[phase, index, :, begin : begin + LANES]
                    packed = jnp.where(lane == 16 * part + place, western[:, LANES - 1 : LANES], packed)
                    packed = jnp.where(lane == 16 * part + 8 + place, eastern[:, 0:1], packed)
        packed = jnp.concatenate([packed, jnp.zeros((stretch - full, LANES), jnp.float32)], axis=0)
        flat = packed.T

        def choose(number, options):
            return jnp.where(number == 0, options[0], jnp.where(number == 1, options[1], options[2]))

        for member in range(3):
            target_row = jnp.clip(row + member - 1, 0, rows_total - 1)
            slot = lax.rem(nest_patch[target_row, col], 9)
            slot_row = lax.div(slot, 3)
            slot_col = lax.rem(slot, 3)
            rows = choose(slot_row, [rim_rows[part] for part in range(3)])
            rim_send[member, 0:16] = choose(
                slot_col, [rows[:, part * patch_cols : (part + 1) * patch_cols] for part in range(3)]
            )
            lines = choose(slot_col, [flat[16 * part : 16 * part + 16] for part in range(3)])
            rim_send[member, 16:32] = choose(
                slot_row, [lines[:, part * patch_rows : part * patch_rows + LANES] for part in range(3)]
            )

            @pl.when(there(member - 1))
            def _():
                rim_copy(member).start()

        choice = [jnp.int32(-1)] * 9
        for member in range(3):
            source = row + member - 1
            entry = nest_patch[jnp.clip(source, 0, rows_total - 1), col]
            valid = all_of([source >= 0, source < rows_total, lax.div(entry, 9) == row])
            for slot in range(9):
                choice[slot] = jnp.where(
                    jnp.logical_and(valid, lax.rem(entry, 9) == slot), jnp.int32(member), choice[slot]
                )

        def up_copy(index):
            return pltpu.make_async_remote_copy(
                src_ref=block_send.at[index],
                dst_ref=block_recv.at[1, index],
                send_sem=up_send_sem.at[index],
                recv_sem=up_recv_sem.at[index],
                device_id=(1 - sec, row, col),
                device_id_type=MESH,
            )

        def side_copy(index, step):
            lane_of = 0 if step < 0 else 1
            return pltpu.make_async_remote_copy(
                src_ref=block_recv.at[1, index],
                dst_ref=block_recv.at[1 - step, index],
                send_sem=side_send_sem.at[lane_of, index],
                recv_sem=side_recv_sem.at[lane_of, index],
                device_id=(sec, row + step, col),
                device_id_type=MESH,
            )

        for step in (-1, 1):

            @pl.when(jnp.logical_not(there(-step)))
            def _():
                block_recv[1 - step] = jnp.zeros(block_recv.shape[1:], jnp.float32)

        for index in range(count):
            up_copy(index).wait_recv()
            for step in (-1, 1):

                @pl.when(there(step))
                def _():
                    side_copy(index, step).start()

        for index in range(count):
            for step in (-1, 1):

                @pl.when(there(-step))
                def _():
                    side_copy(index, step).wait_recv()

            for slot in range(9):
                rows = slice((slot // 3) * patch_rows, (slot // 3 + 1) * patch_rows)
                lanes = slice((slot % 3) * patch_cols, (slot % 3 + 1) * patch_cols)
                own = ext[
                    1, index, top + rows.start : top + rows.stop, left + lanes.start : left + lanes.stop
                ]
                block = own
                for member in range(3):
                    block = jnp.where(choice[slot] == member, block_recv[member, index], block)
                out_ref[index, rows, lanes] = block

        for phase in range(2):
            for direction in range(8):

                @pl.when(there(*DIRECTIONS[direction]))
                def _():
                    halo_copy(phase, direction).wait_send()

        for member in range(3):

            @pl.when(there(member - 1))
            def _():
                rim_copy(member).wait_send()

        for index in range(count):
            for step in (-1, 1):

                @pl.when(there(step))
                def _():
                    side_copy(index, step).wait_send()

    @pl.when(is_nest)
    def _nest():
        for member in range(3):

            @pl.when(there(member - 1))
            def _():
                pltpu.make_async_remote_copy(
                    src_ref=rim_send.at[2 - member],
                    dst_ref=rim_recv.at[member],
                    send_sem=rim_send_sem.at[2 - member],
                    recv_sem=rim_recv_sem.at[member],
                    device_id=(1 - sec, row + member - 1, col),
                    device_id_type=MESH,
                ).wait_recv()

            @pl.when(jnp.logical_not(there(member - 1)))
            def _():
                rim_recv[member] = jnp.zeros(rim_recv.shape[1:], jnp.float32)

        pick = lax.div(nest_patch[row, col], 9) - row + 1
        message = rim_recv[0]
        for member in (1, 2):
            message = jnp.where(pick == member, rim_recv[member], message)
        columns = message[16:32]

        def refine_weights(cells, fine, offset):
            nest = lax.broadcasted_iota(jnp.int32, (cells, fine), 1)
            cell = lax.broadcasted_iota(jnp.int32, (cells, fine), 0) - offset
            delta = nest - 3 * cell - 1
            near = jnp.abs(delta)
            value = jnp.where(near == 0, 3, jnp.where(near == 1, 2, jnp.where(near == 2, 1, 0)))
            return value.astype(jnp.float32)

        row_weights = refine_weights(LANES, width, 0)
        col_weights = refine_weights(LANES, height, PAD_ROWS)
        fine_rows = third * jnp.dot(
            message[0:16], row_weights, precision=lax.Precision.HIGHEST, preferred_element_type=jnp.float32
        )

        def corners(rows, at):
            west = columns[0:8, at : at + 1]
            east = columns[8:16, at : at + 1]
            return (
                rows
                + jnp.where(wide_lane == 0, third * west, 0.0)
                + jnp.where(wide_lane == width - 1, third * east, 0.0)
            )

        upper = corners(fine_rows[0:8], PAD_ROWS - 1)
        lower = corners(fine_rows[8:16], PAD_ROWS + patch_rows)
        column_block = jnp.concatenate([columns, jnp.zeros((LANES - 16, LANES), jnp.float32)], axis=0)
        fine_columns = third * jnp.dot(
            column_block, col_weights, precision=lax.Precision.HIGHEST, preferred_element_type=jnp.float32
        )
        tall_pad = jnp.zeros((LANES, col_send.shape[-1] - height), jnp.float32)
        fine_columns = jnp.concatenate([fine_columns, tall_pad], axis=1).T
        load_force.wait()
        averaging = (
            lax.broadcasted_iota(jnp.int32, (width, patch_cols), 0) // 3
            == lax.broadcasted_iota(jnp.int32, (width, patch_cols), 1)
        ).astype(jnp.bfloat16)

        def blend(old, new, substep):
            return old + (substep / 3.0) * (new - old) if substep else old

        for index in range(count):
            spread = 3.0 * diffusion[index]
            for substep in range(3):
                now = substep % 2
                source = ext.at[now, index]
                at = 2 * index
                source[top - 1 : top, left:right] = blend(upper[at : at + 1], upper[at + 1 : at + 2], substep)
                source[bottom : bottom + 1, left:right] = blend(
                    lower[at : at + 1], lower[at + 1 : at + 2], substep
                )
                west = blend(fine_columns[0:height, at : at + 1], fine_columns[0:height, at + 1 : at + 2], substep)
                east = blend(
                    fine_columns[0:height, 8 + at : 9 + at], fine_columns[0:height, 9 + at : 10 + at], substep
                )

                def store(start, value, substep=substep, now=now, index=index):
                    if substep < 2:
                        ext[1 - now, index, top + start : top + start + chunk, left:right] = value
                    else:
                        out_ref[index, start : start + chunk] = value

                stencil_field(
                    index,
                    source,
                    lambda start: west[start : start + chunk],
                    lambda start: east[start : start + chunk],
                    spread,
                    third,
                    store,
                )
            full = out_ref[index]
            high = full.astype(jnp.bfloat16)
            low = (full - high.astype(jnp.float32)).astype(jnp.bfloat16)
            across = jnp.dot(high, averaging, preferred_element_type=jnp.float32) + jnp.dot(
                low, averaging, preferred_element_type=jnp.float32
            )
            fold[...] = across
            block_send[index] = (1.0 / 9.0) * (
                fold[pl.ds(0, patch_rows, stride=3)]
                + fold[pl.ds(1, patch_rows, stride=3)]
                + fold[pl.ds(2, patch_rows, stride=3)]
            )
            pltpu.make_async_remote_copy(
                src_ref=block_send.at[index],
                dst_ref=block_recv.at[1, index],
                send_sem=up_send_sem.at[index],
                recv_sem=up_recv_sem.at[index],
                device_id=(1 - sec, row, col),
                device_id_type=MESH,
            ).start()
        for index in range(count):
            pltpu.make_async_remote_copy(
                src_ref=block_send.at[index],
                dst_ref=block_recv.at[1, index],
                send_sem=up_send_sem.at[index],
                recv_sem=up_recv_sem.at[index],
                device_id=(1 - sec, row, col),
                device_id_type=MESH,
            ).wait_send()


def on_device(fields, forcing, courant, diffusion, nest_patch):
    _, count, levels, height, width = fields.shape
    own = fields.reshape(count, height, width)
    drive = forcing.reshape(count, height, width)
    rows_total = lax.axis_size("gy")
    cols_total = lax.axis_size("gx")
    patch_rows, patch_cols = height // 3, width // 3
    tall = -(-height // LANES) * LANES
    f32 = jnp.float32
    smem = pl.BlockSpec(memory_space=pltpu.SMEM)
    dma = pltpu.SemaphoreType.DMA
    result = pl.pallas_call(
        functools.partial(kernel, rows_total, cols_total),
        out_shape=jax.ShapeDtypeStruct((count, height, width), f32),
        in_specs=[pl.BlockSpec(memory_space=pl.ANY)] * 2 + [smem] * 3,
        out_specs=pl.BlockSpec(memory_space=pltpu.VMEM),
        scratch_shapes=[
            pltpu.VMEM((2, count, height + 2 * PAD_ROWS, width + 2 * LANES), f32),
            pltpu.VMEM((count, height, width), jnp.bfloat16),
            pltpu.VMEM((2, 2, 8, tall), f32),
            pltpu.VMEM((2, 2, 8, tall), f32),
            pltpu.VMEM((3, 16, width), f32),
            pltpu.VMEM((3, 32, LANES), f32),
            pltpu.VMEM((3, 32, LANES), f32),
            pltpu.VMEM((count, patch_rows, patch_cols), f32),
            pltpu.VMEM((3, count, patch_rows, patch_cols), f32),
            pltpu.VMEM((height, patch_cols), f32),
            dma((2,)),
            dma((2, 8)),
            dma((2, 8)),
            dma((3,)),
            dma((3,)),
            dma((count,)),
            dma((count,)),
            dma((2, count)),
            dma((2, count)),
        ],
        compiler_params=pltpu.CompilerParams(
            collective_id=0, has_side_effects=True, vmem_limit_bytes=40 * 1024 * 1024
        ),
    )(own, drive, courant, diffusion, nest_patch)
    return result.reshape(fields.shape)


def solution(mesh):
    return jax.shard_map(
        on_device,
        mesh=mesh,
        in_specs=(
            P("sec", None, None, "gy", "gx"),
            P("sec", None, None, "gy", "gx"),
            P(),
            P(),
            P(),
        ),
        out_specs=P("sec", None, None, "gy", "gx"),
        check_vma=False,
    )
```

time: 191 us -> 37.4 us (0.20)
  waiting for transfers between devices: 121 us -> 0 us
  starting transfers between devices: 35.1 us -> 0 us
  Pallas kernels: 0 us -> 31.7 us
  other arithmetic: 10.9 us -> 0 us
  between operations: 8.1 us -> 0.01 us
  local copies, waits for them, and re-layouts: 12.4 us -> 5.43 us
    ppermute x14 -> x0, waiting for transfers between devices: 121 us -> none  [the longest x2 101 us: from_behind(): return lax.ppermute(block, axis, route)]
    ppermute x14 -> x0, starting transfers between devices: 35.1 us -> none  [the longest x6 24.8 us: extended(): before = lax.ppermute(last, axis, up)]
    pallas_call x0 -> x1, Pallas kernels: none -> 31.7 us  [on_device(): pl.pallas_call(functools.partial(kernel, rows_total, cols_total), out_sha...]
    broadcast_in_dim x10 -> x0, local copies, waits for them, and re-layouts: 5.67 us -> none  [on_device(): jnp.where(patch_grid == member, arrived[member][:, :, None, :, None, :],...]
    broadcast_in_dim x1 -> x0, other arithmetic: 3.32 us -> none  [on_device(): return result[None]]
    unnamed x13 -> x10, local copies, waits for them, and re-layouts: 2.53 us -> 5.43 us
    concatenate x2 -> x0, other arithmetic: 2.74 us -> none  [extended(): x = jnp.concatenate([before, x, after], axis=dim)]
    dynamic_slice x5 -> x0, local copies, waits for them, and re-layouts: 2.48 us -> none  [the longest x2 1.56 us: pack_rims(): lax.dynamic_slice(padded, (zero, zero, row_start, col_start), (field_coun...]
  transfers between devices with their start and end apart: 14 -> 0, of which waited for: 8 -> 0; matrix products, arithmetic and copies ran while one was open for 1% -> 0% of each run, Pallas kernels for 0% -> 0%
where the time goes in v1:
time: 37.4 us; the launch traced here: 37.2 us
  Pallas kernels  31.7 us (85%)
  local copies, waits for them, and re-layouts  5.43 us (15%)
    pallas_call x1, Pallas kernels, on_device(): pl.pallas_call(functools.partial(kernel, rows_total, cols_total), out_sha...  31.7 us
    unnamed x10, local copies, waits for them, and re-layouts  5.43 us

profile of v1, /device:TPU:0, one launch (start us, length us, event | category | flops | bytes accessed | tf_op | source)
XLA Modules:
  0.0 37.2 jit_solution(8821818178099509721)
XLA Ops:
  0.0 0.7 %copy.6.courant = f32[2,1]{1,0:T(2,128)S(1)} copy(f32[2,1]{0,1:T(1,128)} %param.7) | data formatting | bytes 16 | tf_op args[2]
  0.7 0.0 copy-start
  0.7 1.3 %copy-done = f32[1,4,1,192,384]{4,3,2,1,0:T(8,128)S(1)} copy-done((f32[1,4,1,192,384]{4,3,2,1,0:T(8,128)S(1)}, f32[1,4,1,192,384]{4,3,2,1,0:T(8,128)}, u32[]{:S(2)}) %copy-start) | copy-done | bytes 1179672
  2.0 0.0 copy-start.1
  2.0 1.1 %copy-done.1 = bf16[1,4,1,192,384]{4,3,2,1,0:T(8,128)(2,1)S(1)} copy-done((bf16[1,4,1,192,384]{4,3,2,1,0:T(8,128)(2,1)S(1)}, bf16[1,4,1,192,384]{4,3,2,1,0:T(8,128)(2,1)}, u32[]{:S(2)}) %copy-start.1) | copy-done | bytes 589848
  3.1 0.0 copy-start.2
  3.1 0.7 %copy-done.2 = s32[4,4]{1,0:T(4,128)S(1)} copy-done((s32[4,4]{1,0:T(4,128)S(1)}, s32[4,4]{1,0:T(4,128)}, u32[]{:S(2)}) %copy-start.2) | copy-done | bytes 88
  3.8 0.0 copy-start.3
  3.8 0.7 %copy-done.3 = f32[4]{0:T(128)S(1)} copy-done((f32[4]{0:T(128)S(1)}, f32[4]{0:T(128)}, u32[]{:S(2)}) %copy-start.3) | copy-done | bytes 40
  4.4 31.7 %shard_map.55 = f32[4,192,384]{2,1,0:T(8,128)S(1)} custom-call(f32[4,192,384]{2,1,0:T(8,128)S(1)} %bitcast.6, bf16[4,192,384]{2,1,0:T(8,128)(2,1)S(1)} %bitcast.7, f32[2,1]{1,0:T(2,128)S(1)} %copy.6.courant, f32[4]{0:T(128)S(1)} %copy-done.3, s32[4,4]{1,0:T(4,128)S(1)} %copy-done.2), custom_call_target="tpu_custom_call" | custom-call | tf_op jit(solution)/shard_map/pallas_call | solution.py:521
  36.1 1.0 %copy.9 = f32[1,4,1,192,384]{4,3,2,1,0:T(8,128)} copy(f32[1,4,1,192,384]{4,3,2,1,0:T(8,128)S(1)} %bitcast.5) | data formatting | bytes 2359296
Async XLA Ops:
  0.7 1.3 %copy-start = (f32[1,4,1,192,384]{4,3,2,1,0:T(8,128)S(1)}, f32[1,4,1,192,384]{4,3,2,1,0:T(8,128)}, u32[]{:S(2)}) copy-start(f32[1,4,1,192,384]{4,3,2,1,0:T(8,128)} %param.5) | copy-start | bytes 3538948
  2.0 1.1 %copy-start.1 = (bf16[1,4,1,192,384]{4,3,2,1,0:T(8,128)(2,1)S(1)}, bf16[1,4,1,192,384]{4,3,2,1,0:T(8,128)(2,1)}, u32[]{:S(2)}) copy-start(bf16[1,4,1,192,384]{4,3,2,1,0:T(8,128)(2,1)} %param.6) | copy-start | bytes 1769476
  3.1 0.7 %copy-start.2 = (s32[4,4]{1,0:T(4,128)S(1)}, s32[4,4]{1,0:T(4,128)}, u32[]{:S(2)}) copy-start(s32[4,4]{1,0:T(4,128)} %nest_patch.1) | copy-start | bytes 196
  3.8 0.7 %copy-start.3 = (f32[4]{0:T(128)S(1)}, f32[4]{0:T(128)}, u32[]{:S(2)}) copy-start(f32[4]{0:T(128)} %diffusion.1) | copy-start | bytes 52

commit v2 on v1

--- a/solution.py
+++ b/solution.py
@@ -383,6 +383,35 @@
 
     @pl.when(is_nest)
     def _nest():
+        load_force.wait()
+        for now in range(2):
+            ext[now, :, top - PAD_ROWS : top, left:right] = jnp.zeros((count, PAD_ROWS, width), jnp.float32)
+            ext[now, :, bottom : bottom + PAD_ROWS, left:right] = jnp.zeros(
+                (count, PAD_ROWS, width), jnp.float32
+            )
+
+        def bulk(index, carry):
+            for substep in range(3):
+                now = substep % 2
+
+                def store(start, value, substep=substep, now=now):
+                    if substep < 2:
+                        ext[1 - now, index, top + start : top + start + chunk, left:right] = value
+                    else:
+                        out_ref[index, start : start + chunk] = value
+
+                stencil_field(
+                    index,
+                    ext.at[now, index],
+                    lambda start: 0.0,
+                    lambda start: 0.0,
+                    3.0 * diffusion[index],
+                    third,
+                    store,
+                )
+            return carry
+
+        lax.fori_loop(0, count, bulk, 0)
         for member in range(3):
 
             @pl.when(there(member - 1))
@@ -435,47 +464,75 @@
         fine_columns = third * jnp.dot(
             column_block, col_weights, precision=lax.Precision.HIGHEST, preferred_element_type=jnp.float32
         )
-        tall_pad = jnp.zeros((LANES, col_send.shape[-1] - height), jnp.float32)
-        fine_columns = jnp.concatenate([fine_columns, tall_pad], axis=1).T
-        load_force.wait()
+        tall = col_send.shape[-1]
+        fine_columns = jnp.concatenate(
+            [fine_columns, jnp.zeros((LANES, tall - height), jnp.float32)], axis=1
+        )
         averaging = (
             lax.broadcasted_iota(jnp.int32, (width, patch_cols), 0) // 3
             == lax.broadcasted_iota(jnp.int32, (width, patch_cols), 1)
         ).astype(jnp.bfloat16)
 
-        def blend(old, new, substep):
-            return old + (substep / 3.0) * (new - old) if substep else old
-
+        def strip(old, new, length, at_start, spread, outward, inward, before, after):
+            shape = (8, old.shape[-1])
+            line = lax.broadcasted_iota(jnp.int32, shape, 0)
+            place = lax.broadcasted_iota(jnp.int32, shape, 1)
+            edge, far = (0, 7) if at_start else (7, 0)
+            toward, away = (1, 7) if at_start else (7, 1)
+            value = jnp.zeros(shape, jnp.float32)
+            for substep in range(3):
+                rim = old + (substep / 3.0) * (new - old)
+                outer = jnp.where(line == edge, rim, pltpu.roll(value, toward, 0))
+                inner = jnp.where(line == far, 0.0, pltpu.roll(value, away, 0))
+                previous = jnp.where(place == 0, 0.0, pltpu.roll(value, 1, 1))
+                following = jnp.where(place == length - 1, 0.0, pltpu.roll(value, shape[1] - 1, 1))
+                value = (
+                    (1.0 - 4.0 * spread) * value
+                    + outward * outer
+                    + inward * inner
+                    + before * previous
+                    + after * following
+                )
+                value = jnp.where(place < length, value, 0.0)
+            return value
+
+        sides = [[], []]
         for index in range(count):
             spread = 3.0 * diffusion[index]
-            for substep in range(3):
-                now = substep % 2
-                source = ext.at[now, index]
-                at = 2 * index
-                source[top - 1 : top, left:right] = blend(upper[at : at + 1], upper[at + 1 : at + 2], substep)
-                source[bottom : bottom + 1, left:right] = blend(
-                    lower[at : at + 1], lower[at + 1 : at + 2], substep
+            north, south = spread + half_y, spread - half_y
+            west, east = spread + half_x, spread - half_x
+            at = 2 * index
+            out_ref[index, 0:8] += strip(
+                upper[at : at + 1], upper[at + 1 : at + 2], width, True, spread, north, south, west, east
+            )
+            out_ref[index, height - 8 : height] += strip(
+                lower[at : at + 1], lower[at + 1 : at + 2], width, False, spread, south, north, west, east
+            )
+            for side in range(2):
+                base = 8 * side + at
+                near, beyond = (west, east) if side == 0 else (east, west)
+                sides[side].append(
+                    strip(
+                        fine_columns[base : base + 1],
+                        fine_columns[base + 1 : base + 2],
+                        height,
+                        side == 0,
+                        spread,
+                        near,
+                        beyond,
+                        north,
+                        south,
+                    )
                 )
-                west = blend(fine_columns[0:height, at : at + 1], fine_columns[0:height, at + 1 : at + 2], substep)
-                east = blend(
-                    fine_columns[0:height, 8 + at : 9 + at], fine_columns[0:height, 9 + at : 10 + at], substep
-                )
-
-                def store(start, value, substep=substep, now=now, index=index):
-                    if substep < 2:
-                        ext[1 - now, index, top + start : top + start + chunk, left:right] = value
-                    else:
-                        out_ref[index, start : start + chunk] = value
-
-                stencil_field(
-                    index,
-                    source,
-                    lambda start: west[start : start + chunk],
-                    lambda start: east[start : start + chunk],
-                    spread,
-                    third,
-                    store,
-                )
+        stack = jnp.concatenate(
+            sides[0] + sides[1] + [jnp.zeros((LANES - 16 * count, tall), jnp.float32)], axis=0
+        ).T[0:height]
+        for index in range(count):
+            first = jnp.where(lane < 8, pltpu.roll(stack, (LANES - 8 * index) % LANES, 1), 0.0)
+            shift = (LANES - 8 - 8 * count - 8 * index) % LANES
+            last = jnp.where(lane >= LANES - 8, pltpu.roll(stack, shift, 1), 0.0)
+            out_ref[index, :, 0:LANES] += first
+            out_ref[index, :, width - LANES : width] += last
             full = out_ref[index]
             high = full.astype(jnp.bfloat16)
             low = (full - high.astype(jnp.float32)).astype(jnp.bfloat16)

time: 37.4 us -> 34.6 us (0.925)
  Pallas kernels: 31.7 us -> 29 us
    pallas_call x1, Pallas kernels: 31.7 us -> 29 us  [on_device(): pl.pallas_call(functools.partial(kernel, rows_total, cols_total), out_sha...]
where the time goes in v2:
time: 34.6 us; the launch traced here: 34.4 us
  Pallas kernels  29 us (84%)
  local copies, waits for them, and re-layouts  5.43 us (16%)
    pallas_call x1, Pallas kernels, on_device(): pl.pallas_call(functools.partial(kernel, rows_total, cols_total), out_sha...  29 us
    unnamed x10, local copies, waits for them, and re-layouts  5.43 us

profile of v2, /device:TPU:0, one launch (start us, length us, event | category | flops | bytes accessed | tf_op | source)
XLA Modules:
  0.0 34.4 jit_solution(12736880293346538632)
XLA Ops:
  0.0 0.7 %copy.6.courant = f32[2,1]{1,0:T(2,128)S(1)} copy(f32[2,1]{0,1:T(1,128)} %param.7) | data formatting | bytes 16 | tf_op args[2]
  0.7 0.0 copy-start
  0.7 1.3 %copy-done = f32[1,4,1,192,384]{4,3,2,1,0:T(8,128)S(1)} copy-done((f32[1,4,1,192,384]{4,3,2,1,0:T(8,128)S(1)}, f32[1,4,1,192,384]{4,3,2,1,0:T(8,128)}, u32[]{:S(2)}) %copy-start) | copy-done | bytes 1179672
  2.0 0.0 copy-start.1
  2.0 1.1 %copy-done.1 = bf16[1,4,1,192,384]{4,3,2,1,0:T(8,128)(2,1)S(1)} copy-done((bf16[1,4,1,192,384]{4,3,2,1,0:T(8,128)(2,1)S(1)}, bf16[1,4,1,192,384]{4,3,2,1,0:T(8,128)(2,1)}, u32[]{:S(2)}) %copy-start.1) | copy-done | bytes 589848
  3.1 0.0 copy-start.2
  3.1 0.7 %copy-done.2 = s32[4,4]{1,0:T(4,128)S(1)} copy-done((s32[4,4]{1,0:T(4,128)S(1)}, s32[4,4]{1,0:T(4,128)}, u32[]{:S(2)}) %copy-start.2) | copy-done | bytes 88
  3.8 0.0 copy-start.3
  3.8 0.7 %copy-done.3 = f32[4]{0:T(128)S(1)} copy-done((f32[4]{0:T(128)S(1)}, f32[4]{0:T(128)}, u32[]{:S(2)}) %copy-start.3) | copy-done | bytes 40
  4.4 29.0 %shard_map.55 = f32[4,192,384]{2,1,0:T(8,128)S(1)} custom-call(f32[4,192,384]{2,1,0:T(8,128)S(1)} %bitcast.6, bf16[4,192,384]{2,1,0:T(8,128)(2,1)S(1)} %bitcast.7, f32[2,1]{1,0:T(2,128)S(1)} %copy.6.courant, f32[4]{0:T(128)S(1)} %copy-done.3, s32[4,4]{1,0:T(4,128)S(1)} %copy-done.2), custom_call_target="tpu_custom_call" | custom-call | tf_op jit(solution)/shard_map/pallas_call | solution.py:578
  33.4 1.0 %copy.9 = f32[1,4,1,192,384]{4,3,2,1,0:T(8,128)} copy(f32[1,4,1,192,384]{4,3,2,1,0:T(8,128)S(1)} %bitcast.5) | data formatting | bytes 2359296
Async XLA Ops:
  0.7 1.3 %copy-start = (f32[1,4,1,192,384]{4,3,2,1,0:T(8,128)S(1)}, f32[1,4,1,192,384]{4,3,2,1,0:T(8,128)}, u32[]{:S(2)}) copy-start(f32[1,4,1,192,384]{4,3,2,1,0:T(8,128)} %param.5) | copy-start | bytes 3538948
  2.0 1.1 %copy-start.1 = (bf16[1,4,1,192,384]{4,3,2,1,0:T(8,128)(2,1)S(1)}, bf16[1,4,1,192,384]{4,3,2,1,0:T(8,128)(2,1)}, u32[]{:S(2)}) copy-start(bf16[1,4,1,192,384]{4,3,2,1,0:T(8,128)(2,1)} %param.6) | copy-start | bytes 1769476
  3.1 0.7 %copy-start.2 = (s32[4,4]{1,0:T(4,128)S(1)}, s32[4,4]{1,0:T(4,128)}, u32[]{:S(2)}) copy-start(s32[4,4]{1,0:T(4,128)} %nest_patch.1) | copy-start | bytes 196
  3.8 0.7 %copy-start.3 = (f32[4]{0:T(128)S(1)}, f32[4]{0:T(128)}, u32[]{:S(2)}) copy-start(f32[4]{0:T(128)} %diffusion.1) | copy-start | bytes 52

commit v3 on v2

--- a/solution.py
+++ b/solution.py
@@ -40,6 +40,8 @@
     block_send,
     block_recv,
     fold,
+    ring_send,
+    ring_recv,
     load_sem,
     halo_send_sem,
     halo_recv_sem,
@@ -49,6 +51,8 @@
     up_recv_sem,
     side_send_sem,
     side_recv_sem,
+    ring_send_sem,
+    ring_recv_sem,
 ):
     count, height, width = out_ref.shape
     patch_rows, patch_cols = height // 3, width // 3
@@ -334,6 +338,7 @@
             @pl.when(jnp.logical_not(there(-step)))
             def _():
                 block_recv[1 - step] = jnp.zeros(block_recv.shape[1:], jnp.float32)
+                ring_recv[1 - step] = jnp.zeros(ring_recv.shape[1:], jnp.float32)
 
         for index in range(count):
             up_copy(index).wait_recv()
@@ -343,6 +348,59 @@
                 def _():
                     side_copy(index, step).start()
 
+        def ring_side(step):
+            lane_of = 1 if step < 0 else 2
+            return pltpu.make_async_remote_copy(
+                src_ref=ring_recv.at[1],
+                dst_ref=ring_recv.at[1 - step],
+                send_sem=ring_send_sem.at[lane_of],
+                recv_sem=ring_recv_sem.at[lane_of],
+                device_id=(sec, row + step, col),
+                device_id_type=MESH,
+            )
+
+        pltpu.make_async_remote_copy(
+            src_ref=ring_send,
+            dst_ref=ring_recv.at[1],
+            send_sem=ring_send_sem.at[0],
+            recv_sem=ring_recv_sem.at[0],
+            device_id=(1 - sec, row, col),
+            device_id_type=MESH,
+        ).wait_recv()
+        for step in (-1, 1):
+
+            @pl.when(there(step))
+            def _():
+                ring_side(step).start()
+
+        for step in (-1, 1):
+
+            @pl.when(there(-step))
+            def _():
+                ring_side(step).wait_recv()
+
+        ring_columns = jnp.concatenate(
+            [ring_recv[member, 8:16] for member in range(3)] + [jnp.zeros((LANES - 24, LANES), jnp.float32)],
+            axis=0,
+        ).T
+        block_line = lax.broadcasted_iota(jnp.int32, (patch_rows, 1), 0)
+
+        def corrected(member, index):
+            at = 8 * member + index
+            return (
+                block_recv[member, index]
+                + jnp.where(block_line == 0, ring_recv[member, index : index + 1], 0.0)
+                + jnp.where(
+                    block_line == patch_rows - 1,
+                    ring_recv[member, count + index : count + index + 1],
+                    0.0,
+                )
+                + jnp.where(lane == 0, ring_columns[0:patch_rows, at : at + 1], 0.0)
+                + jnp.where(
+                    lane == patch_cols - 1, ring_columns[0:patch_rows, at + count : at + count + 1], 0.0
+                )
+            )
+
         for index in range(count):
             for step in (-1, 1):
 
@@ -350,6 +408,7 @@
                 def _():
                     side_copy(index, step).wait_recv()
 
+            candidates = [corrected(member, index) for member in range(3)]
             for slot in range(9):
                 rows = slice((slot // 3) * patch_rows, (slot // 3 + 1) * patch_rows)
                 lanes = slice((slot % 3) * patch_cols, (slot % 3 + 1) * patch_cols)
@@ -358,7 +417,7 @@
                 ]
                 block = own
                 for member in range(3):
-                    block = jnp.where(choice[slot] == member, block_recv[member, index], block)
+                    block = jnp.where(choice[slot] == member, candidates[member], block)
                 out_ref[index, rows, lanes] = block
 
         for phase in range(2):
@@ -373,6 +432,12 @@
             @pl.when(there(member - 1))
             def _():
                 rim_copy(member).wait_send()
+
+        for step in (-1, 1):
+
+            @pl.when(there(step))
+            def _():
+                ring_side(step).wait_send()
 
         for index in range(count):
             for step in (-1, 1):
@@ -412,6 +477,31 @@
             return carry
 
         lax.fori_loop(0, count, bulk, 0)
+        averaging = (
+            lax.broadcasted_iota(jnp.int32, (width, patch_cols), 0) // 3
+            == lax.broadcasted_iota(jnp.int32, (width, patch_cols), 1)
+        ).astype(jnp.bfloat16)
+        for index in range(count):
+            full = out_ref[index]
+            high = full.astype(jnp.bfloat16)
+            low = (full - high.astype(jnp.float32)).astype(jnp.bfloat16)
+            across = jnp.dot(high, averaging, preferred_element_type=jnp.float32) + jnp.dot(
+                low, averaging, preferred_element_type=jnp.float32
+            )
+            fold[...] = across
+            block_send[index] = (1.0 / 9.0) * (
+                fold[pl.ds(0, patch_rows, stride=3)]
+                + fold[pl.ds(1, patch_rows, stride=3)]
+                + fold[pl.ds(2, patch_rows, stride=3)]
+            )
+            pltpu.make_async_remote_copy(
+                src_ref=block_send.at[index],
+                dst_ref=block_recv.at[1, index],
+                send_sem=up_send_sem.at[index],
+                recv_sem=up_recv_sem.at[index],
+                device_id=(1 - sec, row, col),
+                device_id_type=MESH,
+            ).start()
         for member in range(3):
 
             @pl.when(there(member - 1))
@@ -468,11 +558,6 @@
         fine_columns = jnp.concatenate(
             [fine_columns, jnp.zeros((LANES, tall - height), jnp.float32)], axis=1
         )
-        averaging = (
-            lax.broadcasted_iota(jnp.int32, (width, patch_cols), 0) // 3
-            == lax.broadcasted_iota(jnp.int32, (width, patch_cols), 1)
-        ).astype(jnp.bfloat16)
-
         def strip(old, new, length, at_start, spread, outward, inward, before, after):
             shape = (8, old.shape[-1])
             line = lax.broadcasted_iota(jnp.int32, shape, 0)
@@ -497,17 +582,22 @@
             return value
 
         sides = [[], []]
+        ring = [[], [], [], []]
         for index in range(count):
             spread = 3.0 * diffusion[index]
             north, south = spread + half_y, spread - half_y
             west, east = spread + half_x, spread - half_x
             at = 2 * index
-            out_ref[index, 0:8] += strip(
+            high_strip = strip(
                 upper[at : at + 1], upper[at + 1 : at + 2], width, True, spread, north, south, west, east
             )
-            out_ref[index, height - 8 : height] += strip(
+            low_strip = strip(
                 lower[at : at + 1], lower[at + 1 : at + 2], width, False, spread, south, north, west, east
             )
+            out_ref[index, 0:8] += high_strip
+            out_ref[index, height - 8 : height] += low_strip
+            ring[0].append(jnp.sum(high_strip, axis=0, keepdims=True))
+            ring[1].append(jnp.sum(low_strip, axis=0, keepdims=True))
             for side in range(2):
                 base = 8 * side + at
                 near, beyond = (west, east) if side == 0 else (east, west)
@@ -524,6 +614,27 @@
                         south,
                     )
                 )
+                ring[2 + side].append(jnp.sum(sides[side][-1], axis=0, keepdims=True))
+        column_averaging = (
+            lax.broadcasted_iota(jnp.int32, (tall, LANES), 0) // 3
+            == lax.broadcasted_iota(jnp.int32, (tall, LANES), 1)
+        ).astype(jnp.float32)
+        for part, weigh in ((0, averaging.astype(jnp.float32)), (1, column_averaging)):
+            ring_send[8 * part : 8 * part + 8] = (1.0 / 9.0) * jnp.dot(
+                jnp.concatenate(ring[2 * part] + ring[2 * part + 1], axis=0),
+                weigh,
+                precision=lax.Precision.HIGHEST,
+                preferred_element_type=jnp.float32,
+            )
+        ring_copy = pltpu.make_async_remote_copy(
+            src_ref=ring_send,
+            dst_ref=ring_recv.at[1],
+            send_sem=ring_send_sem.at[0],
+            recv_sem=ring_recv_sem.at[0],
+            device_id=(1 - sec, row, col),
+            device_id_type=MESH,
+        )
+        ring_copy.start()
         stack = jnp.concatenate(
             sides[0] + sides[1] + [jnp.zeros((LANES - 16 * count, tall), jnp.float32)], axis=0
         ).T[0:height]
@@ -533,26 +644,6 @@
             last = jnp.where(lane >= LANES - 8, pltpu.roll(stack, shift, 1), 0.0)
             out_ref[index, :, 0:LANES] += first
             out_ref[index, :, width - LANES : width] += last
-            full = out_ref[index]
-            high = full.astype(jnp.bfloat16)
-            low = (full - high.astype(jnp.float32)).astype(jnp.bfloat16)
-            across = jnp.dot(high, averaging, preferred_element_type=jnp.float32) + jnp.dot(
-                low, averaging, preferred_element_type=jnp.float32
-            )
-            fold[...] = across
-            block_send[index] = (1.0 / 9.0) * (
-                fold[pl.ds(0, patch_rows, stride=3)]
-                + fold[pl.ds(1, patch_rows, stride=3)]
-                + fold[pl.ds(2, patch_rows, stride=3)]
-            )
-            pltpu.make_async_remote_copy(
-                src_ref=block_send.at[index],
-                dst_ref=block_recv.at[1, index],
-                send_sem=up_send_sem.at[index],
-                recv_sem=up_recv_sem.at[index],
-                device_id=(1 - sec, row, col),
-                device_id_type=MESH,
-            ).start()
         for index in range(count):
             pltpu.make_async_remote_copy(
                 src_ref=block_send.at[index],
@@ -562,6 +653,7 @@
                 device_id=(1 - sec, row, col),
                 device_id_type=MESH,
             ).wait_send()
+        ring_copy.wait_send()
 
 
 def on_device(fields, forcing, courant, diffusion, nest_patch):
@@ -591,6 +683,8 @@
             pltpu.VMEM((count, patch_rows, patch_cols), f32),
             pltpu.VMEM((3, count, patch_rows, patch_cols), f32),
             pltpu.VMEM((height, patch_cols), f32),
+            pltpu.VMEM((16, LANES), f32),
+            pltpu.VMEM((3, 16, LANES), f32),
             dma((2,)),
             dma((2, 8)),
             dma((2, 8)),
@@ -600,6 +694,8 @@
             dma((count,)),
             dma((2, count)),
             dma((2, count)),
+            dma((3,)),
+            dma((3,)),
         ],
         compiler_params=pltpu.CompilerParams(
             collective_id=0, has_side_effects=True, vmem_limit_bytes=40 * 1024 * 1024

time: 34.6 us -> 33.7 us (0.974)
  Pallas kernels: 29 us -> 28 us
    pallas_call x1, Pallas kernels: 29 us -> 28 us  [on_device(): pl.pallas_call(functools.partial(kernel, rows_total, cols_total), out_sha...]
where the time goes in v3:
time: 33.7 us; the launch traced here: 33.5 us
  Pallas kernels  28 us (83%)
  local copies, waits for them, and re-layouts  5.43 us (16%)
    pallas_call x1, Pallas kernels, on_device(): pl.pallas_call(functools.partial(kernel, rows_total, cols_total), out_sha...  28 us
    unnamed x10, local copies, waits for them, and re-layouts  5.43 us

profile of v3, /device:TPU:0, one launch (start us, length us, event | category | flops | bytes accessed | tf_op | source)
XLA Modules:
  0.0 33.5 jit_solution(3220341298577247430)
XLA Ops:
  0.0 0.7 %copy.6.courant = f32[2,1]{1,0:T(2,128)S(1)} copy(f32[2,1]{0,1:T(1,128)} %param.7) | data formatting | bytes 16 | tf_op args[2]
  0.7 0.0 copy-start
  0.7 1.3 %copy-done = f32[1,4,1,192,384]{4,3,2,1,0:T(8,128)S(1)} copy-done((f32[1,4,1,192,384]{4,3,2,1,0:T(8,128)S(1)}, f32[1,4,1,192,384]{4,3,2,1,0:T(8,128)}, u32[]{:S(2)}) %copy-start) | copy-done | bytes 1179672
  2.0 0.0 copy-start.1
  2.0 1.1 %copy-done.1 = bf16[1,4,1,192,384]{4,3,2,1,0:T(8,128)(2,1)S(1)} copy-done((bf16[1,4,1,192,384]{4,3,2,1,0:T(8,128)(2,1)S(1)}, bf16[1,4,1,192,384]{4,3,2,1,0:T(8,128)(2,1)}, u32[]{:S(2)}) %copy-start.1) | copy-done | bytes 589848
  3.1 0.0 copy-start.2
  3.1 0.7 %copy-done.2 = s32[4,4]{1,0:T(4,128)S(1)} copy-done((s32[4,4]{1,0:T(4,128)S(1)}, s32[4,4]{1,0:T(4,128)}, u32[]{:S(2)}) %copy-start.2) | copy-done | bytes 88
  3.8 0.0 copy-start.3
  3.8 0.7 %copy-done.3 = f32[4]{0:T(128)S(1)} copy-done((f32[4]{0:T(128)S(1)}, f32[4]{0:T(128)}, u32[]{:S(2)}) %copy-start.3) | copy-done | bytes 40
  4.4 28.0 %shard_map.55 = f32[4,192,384]{2,1,0:T(8,128)S(1)} custom-call(f32[4,192,384]{2,1,0:T(8,128)S(1)} %bitcast.6, bf16[4,192,384]{2,1,0:T(8,128)(2,1)S(1)} %bitcast.7, f32[2,1]{1,0:T(2,128)S(1)} %copy.6.courant, f32[4]{0:T(128)S(1)} %copy-done.3, s32[4,4]{1,0:T(4,128)S(1)} %copy-done.2), custom_call_target="tpu_custom_call" | custom-call | tf_op jit(solution)/shard_map/pallas_call | solution.py:670
  32.5 1.0 %copy.9 = f32[1,4,1,192,384]{4,3,2,1,0:T(8,128)} copy(f32[1,4,1,192,384]{4,3,2,1,0:T(8,128)S(1)} %bitcast.5) | data formatting | bytes 2359296
Async XLA Ops:
  0.7 1.3 %copy-start = (f32[1,4,1,192,384]{4,3,2,1,0:T(8,128)S(1)}, f32[1,4,1,192,384]{4,3,2,1,0:T(8,128)}, u32[]{:S(2)}) copy-start(f32[1,4,1,192,384]{4,3,2,1,0:T(8,128)} %param.5) | copy-start | bytes 3538948
  2.0 1.1 %copy-start.1 = (bf16[1,4,1,192,384]{4,3,2,1,0:T(8,128)(2,1)S(1)}, bf16[1,4,1,192,384]{4,3,2,1,0:T(8,128)(2,1)}, u32[]{:S(2)}) copy-start(bf16[1,4,1,192,384]{4,3,2,1,0:T(8,128)(2,1)} %param.6) | copy-start | bytes 1769476
  3.1 0.7 %copy-start.2 = (s32[4,4]{1,0:T(4,128)S(1)}, s32[4,4]{1,0:T(4,128)}, u32[]{:S(2)}) copy-start(s32[4,4]{1,0:T(4,128)} %nest_patch.1) | copy-start | bytes 196
  3.8 0.7 %copy-start.3 = (f32[4]{0:T(128)S(1)}, f32[4]{0:T(128)}, u32[]{:S(2)}) copy-start(f32[4]{0:T(128)} %diffusion.1) | copy-start | bytes 52

commit v4 on v3

--- a/solution.py
+++ b/solution.py
@@ -249,7 +249,6 @@
 
         lax.fori_loop(0, count, advance, 0)
         start_exchange(1)
-        end_exchange(1)
 
         def rim_copy(member):
             return pltpu.make_async_remote_copy(
@@ -263,9 +262,9 @@
 
         full = ext.shape[2]
         stretch = 2 * LANES
-        packed = jnp.zeros((full, LANES), jnp.float32)
-        for index in range(count):
-            for phase in range(2):
+
+        def pack_rims(phase, packed):
+            for index in range(count):
                 place = 2 * index + phase
                 for part in range(3):
                     above = top + part * patch_rows - 1
@@ -278,6 +277,11 @@
                     eastern = ext[phase, index, :, begin : begin + LANES]
                     packed = jnp.where(lane == 16 * part + place, western[:, LANES - 1 : LANES], packed)
                     packed = jnp.where(lane == 16 * part + 8 + place, eastern[:, 0:1], packed)
+            return packed
+
+        packed = pack_rims(0, jnp.zeros((full, LANES), jnp.float32))
+        end_exchange(1)
+        packed = pack_rims(1, packed)
         packed = jnp.concatenate([packed, jnp.zeros((stretch - full, LANES), jnp.float32)], axis=0)
         flat = packed.T
 
@@ -670,7 +674,7 @@
     result = pl.pallas_call(
         functools.partial(kernel, rows_total, cols_total),
         out_shape=jax.ShapeDtypeStruct((count, height, width), f32),
-        in_specs=[pl.BlockSpec(memory_space=pl.ANY)] * 2 + [smem] * 3,
+        in_specs=[pl.BlockSpec(memory_space=pltpu.HBM)] * 2 + [smem] * 3,
         out_specs=pl.BlockSpec(memory_space=pltpu.VMEM),
         scratch_shapes=[
             pltpu.VMEM((2, count, height + 2 * PAD_ROWS, width + 2 * LANES), f32),
@@ -698,7 +702,7 @@
             dma((3,)),
         ],
         compiler_params=pltpu.CompilerParams(
-            collective_id=0, has_side_effects=True, vmem_limit_bytes=40 * 1024 * 1024
+            collective_id=0, has_side_effects=True, vmem_limit_bytes=63 * 1024 * 1024
         ),
     )(own, drive, courant, diffusion, nest_patch)
     return result.reshape(fields.shape)

time: 33.7 us -> 32.1 us (0.953)
  local copies, waits for them, and re-layouts: 5.43 us -> 3.66 us
    unnamed x10 -> x2, local copies, waits for them, and re-layouts: 5.43 us -> 3.66 us
where the time goes in v4:
time: 32.1 us; the launch traced here: 31.9 us
  Pallas kernels  28.3 us (88%)
  local copies, waits for them, and re-layouts  3.66 us (11%)
    pallas_call x1, Pallas kernels, on_device(): pl.pallas_call(functools.partial(kernel, rows_total, cols_total), out_sha...  28.3 us
    unnamed x2, local copies, waits for them, and re-layouts  3.66 us

profile of v4, /device:TPU:0, one launch (start us, length us, event | category | flops | bytes accessed | tf_op | source)
XLA Modules:
  0.0 31.9 jit_solution(4545290191415013652)
XLA Ops:
  0.0 1.3 %copy.6.courant = f32[2,1]{1,0:T(2,128)} copy(f32[2,1]{0,1:T(1,128)} %param.7) | data formatting | bytes 16 | tf_op args[2]
  1.3 28.3 %shard_map.55 = f32[4,192,384]{2,1,0:T(8,128)} custom-call(f32[4,192,384]{2,1,0:T(8,128)} %bitcast.6, bf16[4,192,384]{2,1,0:T(8,128)(2,1)} %bitcast.7, f32[2,1]{1,0:T(2,128)} %copy.6.courant, f32[4]{0:T(128)} %diffusion.1, s32[4,4]{1,0:T(4,128)} %nest_patch.1), custom_call_target="tpu_custom_call" | custom-call | tf_op jit(solution)/shard_map/pallas_call | solution.py:674
  29.6 2.4 %copy.9 = f32[1,4,1,192,384]{4,3,2,1,0:T(8,128)} copy(f32[1,4,1,192,384]{4,3,2,1,0:T(8,128)} %bitcast.5) | data formatting | bytes 2359296

commit v5 on v4

--- a/solution.py
+++ b/solution.py
@@ -104,8 +104,8 @@
 
     lane = lax.broadcasted_iota(jnp.int32, (1, LANES), 1)
     wide_lane = lax.broadcasted_iota(jnp.int32, (1, width), 1)
-    half_x = 0.5 * courant[0, 0]
-    half_y = 0.5 * courant[1, 0]
+    half_x = 0.5 * courant[0]
+    half_y = 0.5 * courant[1]
     chunk = 32
 
     def stencil_field(index, source, west_of, east_of, spread, drive_scale, store):
@@ -704,7 +704,7 @@
         compiler_params=pltpu.CompilerParams(
             collective_id=0, has_side_effects=True, vmem_limit_bytes=63 * 1024 * 1024
         ),
-    )(own, drive, courant, diffusion, nest_patch)
+    )(own, drive, courant.reshape(2), diffusion, nest_patch)
     return result.reshape(fields.shape)
 
 

time: 32.1 us -> 30.8 us (0.960)
  local copies, waits for them, and re-layouts: 3.66 us -> 2.36 us
    unnamed x2 -> x1, local copies, waits for them, and re-layouts: 3.66 us -> 2.36 us
where the time goes in v5:
time: 30.8 us; the launch traced here: 30.6 us
  Pallas kernels  28.2 us (92%)
  local copies, waits for them, and re-layouts  2.36 us (8%)
    pallas_call x1, Pallas kernels, on_device(): pl.pallas_call(functools.partial(kernel, rows_total, cols_total), out_sha...  28.2 us
    unnamed x1, local copies, waits for them, and re-layouts  2.36 us

profile of v5, /device:TPU:0, one launch (start us, length us, event | category | flops | bytes accessed | tf_op | source)
XLA Modules:
  0.0 30.6 jit_solution(3248824827222681558)
XLA Ops:
  0.0 28.2 %shard_map.55 = f32[4,192,384]{2,1,0:T(8,128)} custom-call(f32[4,192,384]{2,1,0:T(8,128)} %bitcast.7, bf16[4,192,384]{2,1,0:T(8,128)(2,1)} %bitcast.8, f32[2]{0:T(128)} %bitcast.9, f32[4]{0:T(128)} %diffusion.1, s32[4,4]{1,0:T(4,128)} %nest_patch.1), custom_call_target="tpu_custom_call" | custom-call | tf_op jit(solution)/shard_map/pallas_call | solution.py:674
  28.3 2.4 %copy.8 = f32[1,4,1,192,384]{4,3,2,1,0:T(8,128)} copy(f32[1,4,1,192,384]{4,3,2,1,0:T(8,128)} %bitcast.6) | data formatting | bytes 2359296
